TPU v7x, 512 devices: a whole 4x8x8 slice. The times are simulated.
512 devices in a mesh: row: 64 (over z, y), blk: 8 (over x, core).
Axes of the slice: x: 4, y: 8, z: 8, core: 2. Of those that a mesh axis runs over, the one named last changes fastest.
Arguments:
- matrix: float32 [65536, 2048], P('row', 'blk'), may hold values from -24 to 24, as said below
- sender_slot: int32 [4, 8], P(None, 'blk'), may hold values from 0 to 1
Outputs:
- rotated_matrix: float32 [65536, 2048], P('row', 'blk')
Inputs may be any that keep to these rules, and one draw needn't show every extreme that they name: Each entry of the matrix has a column factor that differs from column to column.
All inputs are finite; a program needn't handle non-finite values.
Results may differ from a plain program's by a relative error of at most 0.0003.
Values sent between devices are 32-bit elements; how exact they have to be, the bound alone decides.
No kernel may reach another device: no remote copies, remote signals or barrier semaphores. Data moves between devices by JAX's collectives and lax.ppermute only.
A program may use at most 64 MiB of HBM per device.

v0:
```python
import jax
import jax.numpy as jnp
from jax import lax
from jax.sharding import PartitionSpec as P

STEPS = 4
ROUNDS = 8


def passed_along(block, axis, distance):
    devices = range(lax.axis_size(axis))
    route = [((i - distance) % len(devices), i) for i in devices]
    return lax.ppermute(block, axis, route)


def exact_dot(left, right):
    return jnp.dot(left, right, precision=lax.Precision.HIGHEST, preferred_element_type=jnp.float32)


def advance(values, axis, period):
    head = lax.slice_in_dim(values, 0, 1, axis=axis)
    middle = lax.slice_in_dim(values, 1, period, axis=axis)
    tail = lax.slice_in_dim(values, period, period + 1, axis=axis)
    return jnp.concatenate([middle, head, tail], axis=axis)


def jacobi_rounds(gram_matrix, offset):
    dimension = gram_matrix.shape[0]
    period = dimension - 1
    position = jnp.arange(dimension, dtype=jnp.int32)
    start_order = jnp.where(position == period, period, jnp.mod(offset + position, period))
    placing = (position[:, None] == start_order[None, :]).astype(jnp.float32)
    laid_out = exact_dot(placing.T, exact_dot(gram_matrix, placing))

    def one_round(round_index, carried):
        current, rotation, order = carried
        is_lower = order < jnp.flip(order)
        own_diag = jnp.diagonal(current)
        other_diag = jnp.flip(own_diag)
        anti_values = jnp.diagonal(jnp.flip(current, 1))
        coupling = jnp.where(is_lower, anti_values, jnp.flip(anti_values))
        difference = jnp.where(is_lower, other_diag - own_diag, own_diag - other_diag)
        sign_term = jnp.where(difference >= 0.0, 1.0, -1.0)
        rotation_angle = 0.5 * jnp.arctan2(2.0 * sign_term * coupling, jnp.abs(difference))
        cosine_term = jnp.cos(rotation_angle)
        sine_term = jnp.where(is_lower, -1.0, 1.0) * jnp.sin(rotation_angle)
        half_turned = current * cosine_term[None, :] + jnp.flip(current, 1) * sine_term[None, :]
        current = cosine_term[:, None] * half_turned + sine_term[:, None] * jnp.flip(half_turned, 0)
        rotation = rotation * cosine_term[None, :] + jnp.flip(rotation, 1) * sine_term[None, :]
        current = advance(advance(current, 0, period), 1, period)
        rotation = advance(rotation, 1, period)
        order = advance(order, 0, period)
        return (current, rotation, order)

    final_h, final_q, final_order = lax.fori_loop(
        0, ROUNDS, one_round, (laid_out, placing, start_order)
    )
    returning = (position[:, None] == final_order[None, :]).astype(jnp.float32)
    rotated_gram = exact_dot(returning, exact_dot(final_h, returning.T))
    rotation = exact_dot(final_q, returning.T)
    return (rotated_gram, rotation)


def inner_products(left_cols, right_cols):
    return lax.dot_general(
        left_cols,
        right_cols,
        (((0,), (0,)), ((), ())),
        precision=lax.Precision.HIGHEST,
        preferred_element_type=jnp.float32,
    )


def apply_rotation(pair_cols, rotation):
    return jnp.dot(
        pair_cols, rotation, precision=lax.Precision.HIGHEST, preferred_element_type=jnp.float32
    )


def send_moved(moved_cols):
    arrived = passed_along(moved_cols, "blk", 1)
    return (arrived, None)


def shards(matrix, sender_slot):
    block_width = matrix.shape[1] // 2
    pair_cols = matrix
    for step_index in range(STEPS):
        gram_matrix = lax.psum(inner_products(pair_cols, pair_cols), "row")
        rotated_gram, rotation = jacobi_rounds(gram_matrix, step_index * ROUNDS)
        chosen = sender_slot[step_index, 0] == 1
        rotated = apply_rotation(pair_cols, rotation)
        moved_cols = jnp.where(chosen, rotated[:, block_width:], rotated[:, :block_width])
        kept_cols = jnp.where(chosen, rotated[:, :block_width], rotated[:, block_width:])
        arrived, tracked = send_moved(moved_cols)
        pair_cols = jnp.concatenate([kept_cols, arrived], axis=1)
    return pair_cols


def solution(mesh):
    return jax.shard_map(
        shards,
        mesh=mesh,
        in_specs=(P("row", "blk"), P(None, "blk")),
        out_specs=P("row", "blk"),
        check_vma=False,
    )
```

profile of v0, /device:TPU:16, one launch (start us, length us, event | category | flops | bytes accessed | tf_op | source)
XLA Modules:
  0.0 966.1 jit_solution(3172175815215367690)
XLA Ops:
  7.8 2.5 fusion.85
  12.3 154.7 %all-reduce.5.cloned.1.call-done = f32[256,256]{1,0:T(8,128)} async-done(((f32[256,256]{1,0:T(8,128)}), f32[256,256]{1,0:T(8,128)}) %all-reduce.5.cloned.1.call-update) | async-done | bytes 262160 | tf_op jit(solution)/shard_map/psum | solution.py:89
  168.6 72.6 %while.56 = (s32[]{:T(128)}, f32[256,256]{1,0:T(8,128)S(1)}, f32[256,256]{1,0:T(8,128)S(1)}, s32[256]{0:T(256)S(1)}, s32[]{:T(128)}) while((s32[]{:T(128)}, f32[256,256]{1,0:T(8,128)S(1)}, f32[256,256]{1,0:T(8,128)S(1)}, s32[256]{0:T(256)S(1)}, s32[]{:T(128)}) %tuple.152), condition=%wide.region_2.3_spmd, body=%wide.region_1.2_spmd.sunk | while | flops 987906 | bytes 7112253 | solution.py:55
  169.0 2.3 gather_fusion
  171.5 2.3 gather_fusion.1
  178.1 2.3 gather_fusion
  180.5 2.3 gather_fusion.1
  187.2 2.3 gather_fusion
  189.6 2.3 gather_fusion.1
  196.2 2.3 gather_fusion
  198.7 2.3 gather_fusion.1
  205.3 2.3 gather_fusion
  207.8 2.3 gather_fusion.1
  214.4 2.3 gather_fusion
  223.4 2.3 gather_fusion
  225.9 2.3 gather_fusion.1
  232.5 2.3 gather_fusion
  235.0 2.3 gather_fusion.1
  243.6 9.8 %collective-permute-done = f32[1024,128]{0,1:T(8,128)S(1)} collective-permute-done((f32[1024,128]{0,1:T(8,128)S(1)}, f32[1024,128]{0,1:T(8,128)S(1)}, u32[]{:S(2)}, u32[]{:S(2)}) %collective-permute-start) | collective-permute-done | bytes 524320 | tf_op jit(solution)/shard_map/ppermute | solution.py:13
  256.1 146.5 %all-reduce.7.cloned.1.call-done = f32[256,256]{1,0:T(8,128)} async-done(((f32[256,256]{1,0:T(8,128)}), f32[256,256]{1,0:T(8,128)}) %all-reduce.7.cloned.1.call-update) | async-done | bytes 262160 | tf_op jit(solution)/shard_map/psum | solution.py:89
  404.2 72.2 %while.57 = (s32[]{:T(128)}, f32[256,256]{1,0:T(8,128)S(1)}, f32[256,256]{1,0:T(8,128)S(1)}, s32[256]{0:T(256)S(1)}, s32[]{:T(128)}) while((s32[]{:T(128)}, f32[256,256]{1,0:T(8,128)S(1)}, f32[256,256]{1,0:T(8,128)S(1)}, s32[256]{0:T(256)S(1)}, s32[]{:T(128)}) %tuple.155), condition=%wide.region_5.6_spmd, body=%wide.region_4.5_spmd.sunk | while | flops 987906 | bytes 7112253 | solution.py:55
  404.6 2.3 gather_fusion.2
  407.0 2.3 gather_fusion.3
  413.6 2.3 gather_fusion.2
  416.1 2.3 gather_fusion.3
  422.6 2.3 gather_fusion.2
  425.1 2.3 gather_fusion.3
  431.7 2.3 gather_fusion.2
  434.1 2.3 gather_fusion.3
  440.7 2.3 gather_fusion.2
  443.1 2.3 gather_fusion.3
  449.7 2.3 gather_fusion.2
  452.2 2.3 gather_fusion.3
  458.7 2.3 gather_fusion.2
  461.2 2.3 gather_fusion.3
  467.8 2.3 gather_fusion.2
  470.2 2.3 gather_fusion.3
  478.7 9.8 %collective-permute-done.1 = f32[1024,128]{0,1:T(8,128)S(1)} collective-permute-done((f32[1024,128]{0,1:T(8,128)S(1)}, f32[1024,128]{0,1:T(8,128)S(1)}, u32[]{:S(2)}, u32[]{:S(2)}) %collective-permute-start.1) | collective-permute-done | bytes 524320 | tf_op jit(solution)/shard_map/ppermute | solution.py:13
  491.2 146.4 %all-reduce.9.cloned.1.call-done = f32[256,256]{1,0:T(8,128)} async-done(((f32[256,256]{1,0:T(8,128)}), f32[256,256]{1,0:T(8,128)}) %all-reduce.9.cloned.1.call-update) | async-done | bytes 262160 | tf_op jit(solution)/shard_map/psum | solution.py:89
  639.3 72.2 %while.58 = (s32[]{:T(128)}, f32[256,256]{1,0:T(8,128)S(1)}, f32[256,256]{1,0:T(8,128)S(1)}, s32[256]{0:T(256)S(1)}, s32[]{:T(128)}) while((s32[]{:T(128)}, f32[256,256]{1,0:T(8,128)S(1)}, f32[256,256]{1,0:T(8,128)S(1)}, s32[256]{0:T(256)S(1)}, s32[]{:T(128)}) %tuple.158), condition=%wide.region_8.9_spmd, body=%wide.region_7.8_spmd.sunk | while | flops 987906 | bytes 7112253 | solution.py:55
  639.7 2.3 gather_fusion.4
  642.1 2.3 gather_fusion.5
  648.7 2.3 gather_fusion.4
  651.2 2.3 gather_fusion.5
  657.7 2.3 gather_fusion.4
  660.2 2.3 gather_fusion.5
  666.8 2.3 gather_fusion.4
  669.2 2.3 gather_fusion.5
  675.8 2.3 gather_fusion.4
  684.8 2.3 gather_fusion.4
  693.8 2.3 gather_fusion.4
  702.8 2.3 gather_fusion.4
  713.8 9.8 %collective-permute-done.2 = f32[1024,128]{0,1:T(8,128)S(1)} collective-permute-done((f32[1024,128]{0,1:T(8,128)S(1)}, f32[1024,128]{0,1:T(8,128)S(1)}, u32[]{:S(2)}, u32[]{:S(2)}) %collective-permute-start.2) | collective-permute-done | bytes 524320 | tf_op jit(solution)/shard_map/ppermute | solution.py:13
  726.0 146.7 %all-reduce.11.cloned.1.call-done = f32[256,256]{1,0:T(8,128)} async-done(((f32[256,256]{1,0:T(8,128)}), f32[256,256]{1,0:T(8,128)}) %all-reduce.11.cloned.1.call-update) | async-done | bytes 262160 | tf_op jit(solution)/shard_map/psum | solution.py:89
  874.4 71.7 %while.59 = (s32[]{:T(128)}, f32[256,256]{1,0:T(8,128)S(1)}, f32[256,256]{1,0:T(8,128)S(1)}, s32[256]{0:T(256)S(1)}, s32[]{:T(128)}) while((s32[]{:T(128)}, f32[256,256]{1,0:T(8,128)S(1)}, f32[256,256]{1,0:T(8,128)S(1)}, s32[256]{0:T(256)S(1)}, s32[]{:T(128)}) %tuple.161), condition=%wide.region_11.12_spmd, body=%wide.region_10.11_spmd.sunk | while | flops 987906 | bytes 7112253 | solution.py:55
  874.8 2.3 gather_fusion.6
  883.7 2.3 gather_fusion.6
  892.7 2.3 gather_fusion.6
  901.7 2.3 gather_fusion.6
  910.6 2.3 gather_fusion.6
  919.6 2.3 gather_fusion.6
  928.5 2.3 gather_fusion.6
  937.5 2.3 gather_fusion.6
  948.4 9.8 %collective-permute-done.3 = f32[1024,128]{0,1:T(8,128)S(1)} collective-permute-done((f32[1024,128]{0,1:T(8,128)S(1)}, f32[1024,128]{0,1:T(8,128)S(1)}, u32[]{:S(2)}, u32[]{:S(2)}) %collective-permute-start.3) | collective-permute-done | bytes 524320 | tf_op jit(solution)/shard_map/ppermute | solution.py:13
  (779 shorter events, 190.9 us)
Async XLA Ops:
  6.5 1.2 copy-start
  6.5 160.4 %all-reduce.5.cloned.1.call-start = ((), (), s32[]{:S(2)}) async-start(), calls=%async_computation | async-start | bytes 524288 | tf_op jit(solution)/shard_map/psum | solution.py:89
  10.3 0.7 copy-start.7
  10.3 392.2 %all-reduce.7.cloned.1.call-start = ((), (), s32[]{:S(2)}) async-start(), calls=%async_computation.1 | async-start | bytes 524288 | tf_op jit(solution)/shard_map/psum | solution.py:89
  243.5 9.8 %collective-permute-start = (f32[1024,128]{0,1:T(8,128)S(1)}, f32[1024,128]{0,1:T(8,128)S(1)}, u32[]{:S(2)}, u32[]{:S(2)}) collective-permute-start(f32[1024,128]{0,1:T(8,128)S(1)} %get-tuple-element.204), channel_id=1, source_target_pairs={{7,0},{0,1},{1,2},{2,3},{3,4},{4,5},{5,6},{6,7},{15,8},{8,9},{9,10... | collective-permute-start | bytes 1572872 | tf_op jit(solution)/shard_map/ppermute | solution.py:13
  253.4 1.8 copy-start.1
  255.2 382.5 %all-reduce.9.cloned.1.call-start = ((), (), s32[]{:S(2)}) async-start(), calls=%async_computation.2 | async-start | bytes 524288 | tf_op jit(solution)/shard_map/psum | solution.py:89
  476.4 1.0 copy-start.2
  478.7 9.8 %collective-permute-start.1 = (f32[1024,128]{0,1:T(8,128)S(1)}, f32[1024,128]{0,1:T(8,128)S(1)}, u32[]{:S(2)}, u32[]{:S(2)}) collective-permute-start(f32[1024,128]{0,1:T(8,128)S(1)} %get-tuple-element.202), channel_id=1, source_target_pairs={{7,0},{0,1},{1,2},{2,3},{3,4},{4,5},{5,6},{6,7},{15,8},{8,9},{9,10... | collective-permute-start | bytes 1572872 | tf_op jit(solution)/shard_map/ppermute | solution.py:13
  488.5 1.8 copy-start.3
  490.3 382.5 %all-reduce.11.cloned.1.call-start = ((), (), s32[]{:S(2)}) async-start(), calls=%async_computation.3 | async-start | bytes 524288 | tf_op jit(solution)/shard_map/psum | solution.py:89
  711.5 1.0 copy-start.4
  713.8 9.8 %collective-permute-start.2 = (f32[1024,128]{0,1:T(8,128)S(1)}, f32[1024,128]{0,1:T(8,128)S(1)}, u32[]{:S(2)}, u32[]{:S(2)}) collective-permute-start(f32[1024,128]{0,1:T(8,128)S(1)} %get-tuple-element.200), channel_id=1, source_target_pairs={{7,0},{0,1},{1,2},{2,3},{3,4},{4,5},{5,6},{6,7},{15,8},{8,9},{9,10... | collective-permute-start | bytes 1572872 | tf_op jit(solution)/shard_map/ppermute | solution.py:13
  723.6 1.8 copy-start.5
  946.1 1.0 copy-start.6
  948.4 9.8 %collective-permute-start.3 = (f32[1024,128]{0,1:T(8,128)S(1)}, f32[1024,128]{0,1:T(8,128)S(1)}, u32[]{:S(2)}, u32[]{:S(2)}) collective-permute-start(f32[1024,128]{0,1:T(8,128)S(1)} %get-tuple-element.198), channel_id=1, source_target_pairs={{7,0},{0,1},{1,2},{2,3},{3,4},{4,5},{5,6},{6,7},{15,8},{8,9},{9,10... | collective-permute-start | bytes 1572872 | tf_op jit(solution)/shard_map/ppermute | solution.py:13
Sparse Core Ops, SparseCore 0:
  10.6 156.3 all-reduce.4
  255.3 147.2 all-reduce.6
  490.4 147.2 all-reduce.8
  725.5 147.1 all-reduce.10
where the time goes:
time: 967 us; the launch traced here: 966 us
  waiting for transfers between devices  634 us (66%)
  local copies, waits for them, and re-layouts  230 us (24%)
  other arithmetic  61.7 us (6%)
  matrix products  20.9 us (2%)
  between operations  15.9 us (2%)
    psum x4, waiting for transfers between devices, shards(): gram_matrix = lax.psum(inner_products(pair_cols, pair_cols), 'row')  594 us
    gather x32, local copies, waits for them, and re-layouts, one_round(): anti_values = jnp.diagonal(jnp.flip(current, 1))  75 us
    gather x32, local copies, waits for them, and re-layouts, one_round(): own_diag = jnp.diagonal(current)  74.9 us
    concatenate x96, other arithmetic, advance(): return jnp.concatenate([middle, head, tail], axis=axis)  50 us
    ppermute x4, waiting for transfers between devices, passed_along(): return lax.ppermute(block, axis, route)  39.2 us
    slice x128, local copies, waits for them, and re-layouts, advance(): head = lax.slice_in_dim(values, 0, 1, axis=axis)  25.9 us
  transfers between devices with their start and end apart: 8, of which 8 were waited for; matrix products, arithmetic and copies ran while one was open for 0% of the time, Pallas kernels for 0%

commit v1 on v0

v1 whole, which is shorter than its diff:
```python
import functools

import jax
import jax.numpy as jnp
from jax import lax
from jax.experimental import pallas as pl
from jax.experimental.pallas import tpu as pltpu
from jax.sharding import PartitionSpec as P

STEPS = 4
ROUNDS = 8
N = 256
HALF = 128
PERIOD = N - 1


def dot(left, right, over=(1, 0)):
    return lax.dot_general(
        left,
        right,
        (((over[0],), (over[1],)), ((), ())),
        precision=lax.Precision.HIGHEST,
        preferred_element_type=jnp.float32,
    )


def seats(position, round_index):
    upper = position + round_index
    upper = jnp.where(upper >= PERIOD, upper - PERIOD, upper)
    lower = round_index - (position - HALF)
    lower = jnp.where(lower < 0, lower + PERIOD, lower)
    return jnp.where(position < HALF, upper, jnp.where(position == HALF, PERIOD, lower))


def placing(round_index):
    index = lax.broadcasted_iota(jnp.int32, (N, N), 0)
    position = lax.broadcasted_iota(jnp.int32, (N, N), 1)
    return (index == seats(position, round_index)).astype(jnp.float32)


def rotations(upper_diag, coupling, lower_diag, round_index):
    position = lax.broadcasted_iota(jnp.int32, (1, HALF), 1)
    is_lower = seats(position, round_index) < seats(position + HALF, round_index)
    difference = jnp.where(is_lower, lower_diag - upper_diag, upper_diag - lower_diag)
    x = jnp.abs(difference)
    y = jnp.where(difference >= 0.0, 2.0 * coupling, -2.0 * coupling)
    largest = jnp.maximum(x, jnp.abs(y))
    scale = jnp.where(largest > 0.0, largest, 1.0)
    x = jnp.where(largest > 0.0, x / scale, 1.0)
    y = y / scale
    tangent = y / (x + jnp.sqrt(x * x + y * y))
    cosine = 1.0 / jnp.sqrt(1.0 + tangent * tangent)
    sine = tangent * cosine
    return cosine, jnp.where(is_lower, -sine, sine)


def turn(upper, lower, cosine, sine):
    return cosine * upper + sine * lower, cosine * lower - sine * upper


def shift(upper, lower, axis):
    at = lax.broadcasted_iota(jnp.int32, upper.shape, axis)
    new_upper = jnp.where(at == HALF - 1, lower, pltpu.roll(upper, HALF - 1, axis))
    moved = pltpu.roll(jnp.where(at == 0, upper, lower), 1, axis)
    return new_upper, jnp.where(at == 0, lower, moved)


def jacobi(gram, offset, parts):
    uu, ul, lu, ll, qu, ql = parts
    start = placing(offset)
    laid_out = dot(start, dot(gram, start), (0, 0))
    uu[...] = laid_out[:HALF, :HALF]
    ul[...] = laid_out[:HALF, HALF:]
    lu[...] = laid_out[HALF:, :HALF]
    ll[...] = laid_out[HALF:, HALF:]
    qu[...] = start[:, :HALF]
    ql[...] = start[:, HALF:]
    shape = (HALF, HALF)
    eye = lax.broadcasted_iota(jnp.int32, shape, 0) == lax.broadcasted_iota(jnp.int32, shape, 1)

    def diagonal(ref):
        return jnp.sum(jnp.where(eye, ref[...], 0.0), axis=0, keepdims=True)

    def stood(row):
        return jnp.sum(jnp.where(eye, jnp.broadcast_to(row, shape), 0.0), axis=1, keepdims=True)

    for round_index in range(offset, offset + ROUNDS):
        cosine, sine = rotations(diagonal(uu), diagonal(ul), diagonal(ll), round_index)
        cosine_col, sine_col = stood(cosine), stood(sine)
        a, b = shift(*turn(uu[...], ul[...], cosine, sine), 1)
        c, d = shift(*turn(lu[...], ll[...], cosine, sine), 1)
        uu[...], lu[...] = shift(*turn(a, c, cosine_col, sine_col), 0)
        ul[...], ll[...] = shift(*turn(b, d, cosine_col, sine_col), 0)
        qu[...], ql[...] = shift(*turn(qu[...], ql[...], cosine, sine), 1)
    end = placing(offset + ROUNDS)
    rotation = dot(jnp.concatenate([qu[...], ql[...]], axis=1), end, (1, 1))
    upper = jnp.concatenate([uu[...], ul[...]], axis=1)
    lower = jnp.concatenate([lu[...], ll[...]], axis=1)
    rotated_gram = dot(end, dot(jnp.concatenate([upper, lower], axis=0), end, (1, 1)))
    return rotation, rotated_gram


def jacobi_kernel(offset, gram, rotation, rotated_gram, *parts):
    rotation[...], rotated_gram[...] = jacobi(gram[...], offset, parts)


def jacobi_rounds(gram, offset):
    square = jax.ShapeDtypeStruct((N, N), jnp.float32)
    return pl.pallas_call(
        functools.partial(jacobi_kernel, offset),
        out_shape=[square, square],
        scratch_shapes=[pltpu.VMEM((HALF, HALF), jnp.float32)] * 4 + [pltpu.VMEM((N, HALF), jnp.float32)] * 2,
        compiler_params=pltpu.CompilerParams(vmem_limit_bytes=16 * 2**20),
    )(gram)


def summed(partial, axis):
    count = lax.axis_size(axis)
    rows, columns = partial.shape
    pieces = partial.reshape(count, rows // count, columns)
    own = jnp.sum(lax.all_to_all(pieces, axis, 0, 0, tiled=True), axis=0)
    spread = jnp.broadcast_to(own[None], pieces.shape)
    return lax.all_to_all(spread, axis, 0, 0, tiled=True).reshape(rows, columns)


def shards(matrix, sender_slot):
    devices = lax.axis_size("blk")
    route = [((i - 1) % devices, i) for i in range(devices)]
    pair_cols = matrix
    gram = summed(dot(matrix, matrix, (0, 0)), "row")
    for step in range(STEPS):
        rotation, rotated_gram = jacobi_rounds(gram, step * ROUNDS)
        second = sender_slot[step, 0] == 1

        def halves(values):
            first_half, second_half = values[:, :HALF], values[:, HALF:]
            return jnp.where(second, first_half, second_half), jnp.where(second, second_half, first_half)

        keep, move = halves(rotation)
        arrived = lax.ppermute(dot(pair_cols, move), "blk", route)
        kept = dot(pair_cols, keep)
        pair_cols = jnp.concatenate([kept, arrived], axis=1)
        if step + 1 < STEPS:
            keep_rows, move_rows = halves(rotated_gram.T)
            moved_gram = lax.ppermute(halves(move_rows.T)[1], "blk", route)
            kept_gram = halves(keep_rows.T)[0]
            cross = summed(dot(kept, arrived, (0, 0)), "row")
            upper = jnp.concatenate([kept_gram, cross], axis=1)
            lower = jnp.concatenate([cross.T, moved_gram], axis=1)
            gram = jnp.concatenate([upper, lower], axis=0)
    return pair_cols


def solution(mesh):
    return jax.shard_map(
        shards,
        mesh=mesh,
        in_specs=(P("row", "blk"), P(None, "blk")),
        out_specs=P("row", "blk"),
        check_vma=False,
    )
```

time: 967 us -> 228 us (0.24)
  the two profiles are of different devices: /device:TPU:16 before, /device:TPU:8 now
where the time goes in v1:
time: 228 us; the launch traced here: 227 us
  waiting for transfers between devices  114 us (50%)
  starting transfers between devices  37.4 us (16%)
  blocking collectives  30.7 us (13%)
  Pallas kernels  22.1 us (10%)
  matrix products  12.2 us (5%)
  local copies, waits for them, and re-layouts  6.97 us (3%)
  between operations  3.06 us (1%)
    all_to_all x4, waiting for transfers between devices, summed(): return lax.all_to_all(spread, axis, 0, 0, tiled=True).reshape(rows, columns)  46.5 us
    all_to_all x3, waiting for transfers between devices, summed(): own = jnp.sum(lax.all_to_all(pieces, axis, 0, 0, tiled=True), axis=0)  34.3 us
    ppermute x4, waiting for transfers between devices, shards(): arrived = lax.ppermute(dot(pair_cols, move), 'blk', route)  32.9 us
    all_to_all x1, blocking collectives, summed(): own = jnp.sum(lax.all_to_all(pieces, axis, 0, 0, tiled=True), axis=0)  30.7 us
    pallas_call x4, Pallas kernels, jacobi_rounds(): pl.pallas_call(functools.partial(jacobi_kernel, offset), out_shape=[squar...  22.1 us
    all_to_all x4, starting transfers between devices, summed(): return lax.all_to_all(spread, axis, 0, 0, tiled=True).reshape(rows, columns)  21.5 us
    all_to_all x3, starting transfers between devices, summed(): own = jnp.sum(lax.all_to_all(pieces, axis, 0, 0, tiled=True), axis=0)  15.8 us
    dot_general x12, matrix products, dot(): lax.dot_general(left, right, (((over[0],), (over[1],)), ((), ())), precis...  12.2 us
  transfers between devices with their start and end apart: 14, of which 11 were waited for; matrix products, arithmetic and copies ran while one was open for 3% of the time, Pallas kernels for 0%

profile of v1, /device:TPU:8, one launch (start us, length us, event | category | flops | bytes accessed | tf_op | source)
XLA Modules:
  0.0 227.5 jit_solution(18098589355060457682)
XLA Ops:
  0.0 1.2 copy-done
  1.2 1.8 fusion.46
  3.1 0.1 reshape.36
  3.2 30.7 %all_to_all.40 = f32[64,4,256]{2,1,0:T(4,128)S(1)} all-to-all(f32[64,4,256]{2,1,0:T(4,128)S(1)} %reshape.36), channel_id=1, replica_groups=mesh['row'=64,'blk'=8] {'row'}, dimensions={0} | all-to-all | bytes 524288 | tf_op jit(solution)/shard_map/all_to_all | solution.py:121
  33.9 0.1 reduce_sum.36
  33.9 0.7 broadcast_in_dim.8
  34.7 5.2 %all-to-all-start.1 = ((f32[64,4,256]{2,1,0:T(4,128)}), f32[64,4,256]{2,1,0:T(4,128)S(1)}, u32[]{:S(2)}, u32[]{:S(2)}) async-start(f32[64,4,256]{2,1,0:T(4,128)} %broadcast_in_dim.8), calls=%async_computation.1 | async-start | bytes 524288 | tf_op jit(solution)/shard_map/all_to_all | solution.py:123
  39.9 0.7 fusion.45
  41.3 12.1 %all-to-all-done.1 = f32[64,4,256]{2,1,0:T(4,128)S(1)} async-done(((f32[64,4,256]{2,1,0:T(4,128)}), f32[64,4,256]{2,1,0:T(4,128)S(1)}, u32[]{:S(2)}, u32[]{:S(2)}) %all-to-all-start.1) | async-done | bytes 262176 | tf_op jit(solution)/shard_map/all_to_all | solution.py:123
  53.4 0.1 reshape.37.gram
  53.5 5.3 %shard_map.28 = (f32[256,256]{1,0:T(8,128)S(1)}, f32[256,256]{1,0:T(8,128)S(1)}) custom-call(f32[256,256]{1,0:T(8,128)S(1)} %reshape.37.gram), custom_call_target="tpu_custom_call" | custom-call | tf_op jit(solution)/shard_map/pallas_call | solution.py:109
  58.9 0.1 copy.3
  59.0 1.2 convolution_bitcast_fusion
  60.2 0.0 collective-permute-start
  60.9 1.2 fusion.13
  62.1 7.9 %collective-permute-done = f32[1024,128]{0,1:T(8,128)S(1)} collective-permute-done((f32[1024,128]{0,1:T(8,128)S(1)}, f32[1024,128]{0,1:T(8,128)S(1)}, u32[]{:S(2)}, u32[]{:S(2)}) %collective-permute-start) | collective-permute-done | bytes 524320 | tf_op jit(solution)/shard_map/ppermute | solution.py:140
  70.1 1.2 fusion.47
  71.3 5.0 %all-to-all-start.2 = ((f32[64,2,128]{2,1,0:T(2,128)}), f32[64,2,128]{2,1,0:T(2,128)S(1)}, u32[]{:S(2)}, u32[]{:S(2)}) async-start(f32[64,2,128]{2,1,0:T(2,128)} %bitcast.6), calls=%async_computation.2 | async-start | bytes 131072 | tf_op jit(solution)/shard_map/all_to_all | solution.py:121
  76.3 0.0 collective-permute-start.1
  76.3 11.4 %all-to-all-done.2 = f32[64,2,128]{2,1,0:T(2,128)S(1)} async-done(((f32[64,2,128]{2,1,0:T(2,128)}), f32[64,2,128]{2,1,0:T(2,128)S(1)}, u32[]{:S(2)}, u32[]{:S(2)}) %all-to-all-start.2) | async-done | bytes 65568 | tf_op jit(solution)/shard_map/all_to_all | solution.py:121
  87.8 0.1 reduce_sum.37
  87.8 0.6 broadcast_in_dim.9
  88.5 5.5 %all-to-all-start.3 = ((f32[64,2,128]{2,1,0:T(2,128)}), f32[64,2,128]{2,1,0:T(2,128)S(1)}, u32[]{:S(2)}, u32[]{:S(2)}) async-start(f32[64,2,128]{2,1,0:T(2,128)} %broadcast_in_dim.9), calls=%async_computation.3 | async-start | bytes 131072 | tf_op jit(solution)/shard_map/all_to_all | solution.py:123
  94.0 11.5 %all-to-all-done.3 = f32[64,2,128]{2,1,0:T(2,128)S(1)} async-done(((f32[64,2,128]{2,1,0:T(2,128)}), f32[64,2,128]{2,1,0:T(2,128)S(1)}, u32[]{:S(2)}, u32[]{:S(2)}) %all-to-all-start.3) | async-done | bytes 65568 | tf_op jit(solution)/shard_map/all_to_all | solution.py:123
  105.5 0.1 copy.5
  105.7 5.4 %shard_map.29 = (f32[256,256]{1,0:T(8,128)S(1)}, f32[256,256]{1,0:T(8,128)S(1)}) custom-call(f32[256,256]{1,0:T(8,128)S(1)} %maximum_maximum_fusion.gram), custom_call_target="tpu_custom_call" | custom-call | tf_op jit(solution)/shard_map/pallas_call | solution.py:109
  111.0 0.1 copy.6
  111.2 0.7 fusion.4
  111.9 0.0 collective-permute-start.2
  112.7 0.3 copy-done.2
  112.9 0.7 fusion.5
  113.7 8.1 %collective-permute-done.2 = f32[1024,128]{0,1:T(8,128)S(1)} collective-permute-done((f32[1024,128]{0,1:T(8,128)S(1)}, f32[1024,128]{0,1:T(8,128)S(1)}, u32[]{:S(2)}, u32[]{:S(2)}) %collective-permute-start.2) | collective-permute-done | bytes 524320 | tf_op jit(solution)/shard_map/ppermute | solution.py:140
  121.7 1.2 fusion.48
  122.9 5.3 %all-to-all-start.4 = ((f32[64,2,128]{2,1,0:T(2,128)}), f32[64,2,128]{2,1,0:T(2,128)S(1)}, u32[]{:S(2)}, u32[]{:S(2)}) async-start(f32[64,2,128]{2,1,0:T(2,128)} %bitcast.13), calls=%async_computation.4 | async-start | bytes 131072 | tf_op jit(solution)/shard_map/all_to_all | solution.py:121
  128.3 0.0 collective-permute-start.3
  128.3 11.5 %all-to-all-done.4 = f32[64,2,128]{2,1,0:T(2,128)S(1)} async-done(((f32[64,2,128]{2,1,0:T(2,128)}), f32[64,2,128]{2,1,0:T(2,128)S(1)}, u32[]{:S(2)}, u32[]{:S(2)}) %all-to-all-start.4) | async-done | bytes 65568 | tf_op jit(solution)/shard_map/all_to_all | solution.py:121
  139.8 0.1 reduce_sum.38
  139.9 0.7 broadcast_in_dim.10
  140.5 5.4 %all-to-all-start.5 = ((f32[64,2,128]{2,1,0:T(2,128)}), f32[64,2,128]{2,1,0:T(2,128)S(1)}, u32[]{:S(2)}, u32[]{:S(2)}) async-start(f32[64,2,128]{2,1,0:T(2,128)} %broadcast_in_dim.10), calls=%async_computation.5 | async-start | bytes 131072 | tf_op jit(solution)/shard_map/all_to_all | solution.py:123
  145.9 11.5 %all-to-all-done.5 = f32[64,2,128]{2,1,0:T(2,128)S(1)} async-done(((f32[64,2,128]{2,1,0:T(2,128)}), f32[64,2,128]{2,1,0:T(2,128)S(1)}, u32[]{:S(2)}, u32[]{:S(2)}) %all-to-all-start.5) | async-done | bytes 65568 | tf_op jit(solution)/shard_map/all_to_all | solution.py:123
  157.4 0.1 copy.9
  157.5 5.4 %shard_map.30 = (f32[256,256]{1,0:T(8,128)S(1)}, f32[256,256]{1,0:T(8,128)S(1)}) custom-call(f32[256,256]{1,0:T(8,128)S(1)} %maximum_maximum_fusion.1.gram), custom_call_target="tpu_custom_call" | custom-call | tf_op jit(solution)/shard_map/pallas_call | solution.py:109
  162.9 0.1 copy.10
  163.0 0.7 fusion.2
  163.7 0.0 collective-permute-start.4
  164.3 0.7 select_bitcast_fusion.1
  165.0 0.7 fusion.3
  165.7 7.8 %collective-permute-done.4 = f32[1024,128]{0,1:T(8,128)S(1)} collective-permute-done((f32[1024,128]{0,1:T(8,128)S(1)}, f32[1024,128]{0,1:T(8,128)S(1)}, u32[]{:S(2)}, u32[]{:S(2)}) %collective-permute-start.4) | collective-permute-done | bytes 524320 | tf_op jit(solution)/shard_map/ppermute | solution.py:140
  173.5 1.2 fusion.49
  174.8 5.4 %all-to-all-start.6 = ((f32[64,2,128]{2,1,0:T(2,128)}), f32[64,2,128]{2,1,0:T(2,128)S(1)}, u32[]{:S(2)}, u32[]{:S(2)}) async-start(f32[64,2,128]{2,1,0:T(2,128)} %bitcast.20), calls=%async_computation.6 | async-start | bytes 131072 | tf_op jit(solution)/shard_map/all_to_all | solution.py:121
  180.2 0.0 collective-permute-start.5
  180.2 11.4 %all-to-all-done.6 = f32[64,2,128]{2,1,0:T(2,128)S(1)} async-done(((f32[64,2,128]{2,1,0:T(2,128)}), f32[64,2,128]{2,1,0:T(2,128)S(1)}, u32[]{:S(2)}, u32[]{:S(2)}) %all-to-all-start.6) | async-done | bytes 65568 | tf_op jit(solution)/shard_map/all_to_all | solution.py:121
  191.7 0.1 reduce_sum.39
  191.8 0.7 broadcast_in_dim.11
  192.4 5.4 %all-to-all-start.7 = ((f32[64,2,128]{2,1,0:T(2,128)}), f32[64,2,128]{2,1,0:T(2,128)S(1)}, u32[]{:S(2)}, u32[]{:S(2)}) async-start(f32[64,2,128]{2,1,0:T(2,128)} %broadcast_in_dim.11), calls=%async_computation.7 | async-start | bytes 131072 | tf_op jit(solution)/shard_map/all_to_all | solution.py:123
  197.8 11.5 %all-to-all-done.7 = f32[64,2,128]{2,1,0:T(2,128)S(1)} async-done(((f32[64,2,128]{2,1,0:T(2,128)}), f32[64,2,128]{2,1,0:T(2,128)S(1)}, u32[]{:S(2)}, u32[]{:S(2)}) %all-to-all-start.7) | async-done | bytes 65568 | tf_op jit(solution)/shard_map/all_to_all | solution.py:123
  209.3 0.1 copy.13
  209.4 6.1 %shard_map.31 = (f32[256,256]{1,0:T(8,128)S(1)}, f32[256,256]{1,0:T(8,128)}) custom-call(f32[256,256]{1,0:T(8,128)S(1)} %maximum_maximum_fusion.2.gram), custom_call_target="tpu_custom_call" | custom-call | tf_op jit(solution)/shard_map/pallas_call | solution.py:109
  215.5 0.7 fusion
  216.2 0.0 collective-permute-start.6
  216.2 0.7 fusion.1
  217.0 9.0 %collective-permute-done.6 = f32[1024,128]{0,1:T(8,128)S(1)} collective-permute-done((f32[1024,128]{0,1:T(8,128)S(1)}, f32[1024,128]{0,1:T(8,128)S(1)}, u32[]{:S(2)}, u32[]{:S(2)}) %collective-permute-start.6) | collective-permute-done | bytes 524320 | tf_op jit(solution)/shard_map/ppermute | solution.py:140
  226.1 0.1 pad_maximum_fusion.3
  226.2 1.3 copy.15
  (22 shorter events, 0.2 us)
Async XLA Ops:
  0.0 1.2 copy-start
  34.7 5.3 %copy-start.4 = (s32[4,1]{0,1:T(1,128)S(1)}, s32[4,1]{0,1:T(1,128)}, u32[]{:S(2)}) copy-start(s32[4,1]{0,1:T(1,128)} %param.3) | copy-start | bytes 52
  34.7 18.7 %all-to-all-start.1 = ((f32[64,4,256]{2,1,0:T(4,128)}), f32[64,4,256]{2,1,0:T(4,128)S(1)}, u32[]{:S(2)}, u32[]{:S(2)}) async-start(f32[64,4,256]{2,1,0:T(4,128)} %broadcast_in_dim.8), calls=%async_computation.1 | async-start | bytes 524288 | tf_op jit(solution)/shard_map/all_to_all | solution.py:123
  60.2 9.8 %collective-permute-start = (f32[1024,128]{0,1:T(8,128)S(1)}, f32[1024,128]{0,1:T(8,128)S(1)}, u32[]{:S(2)}, u32[]{:S(2)}) collective-permute-start(f32[1024,128]{0,1:T(8,128)S(1)} %convolution_bitcast_fusion), channel_id=1, source_target_pairs={{7,0},{0,1},{1,2},{2,3},{3,4},{4,5},{5,6},{6,7},{15,8},{8,9},{9,10... | collective-permute-start | bytes 1572872 | tf_op jit(solution)/shard_map/ppermute | solution.py:140
  70.0 41.1 %copy-start.1 = (f32[1024,128]{0,1:T(8,128)}, f32[1024,128]{0,1:T(8,128)S(1)}, u32[]{:S(2)}) copy-start(f32[1024,128]{0,1:T(8,128)S(1)} %collective-permute-done) | copy-start | bytes 1572868
  71.3 16.5 %all-to-all-start.2 = ((f32[64,2,128]{2,1,0:T(2,128)}), f32[64,2,128]{2,1,0:T(2,128)S(1)}, u32[]{:S(2)}, u32[]{:S(2)}) async-start(f32[64,2,128]{2,1,0:T(2,128)} %bitcast.6), calls=%async_computation.2 | async-start | bytes 131072 | tf_op jit(solution)/shard_map/all_to_all | solution.py:121
  76.3 29.3 %collective-permute-start.1 = (f32[128,128]{1,0:T(8,128)S(1)}, f32[128,128]{1,0:T(8,128)S(1)}, u32[]{:S(2)}, u32[]{:S(2)}) collective-permute-start(f32[128,128]{1,0:T(8,128)S(1)} %slice_select_fusion.4), channel_id=1, source_target_pairs={{7,0},{0,1},{1,2},{2,3},{3,4},{4,5},{5,6},{6,7},{15,8},{8,9},{9,10... | collective-permute-start | bytes 196616 | tf_op jit(solution)/shard_map/ppermute | solution.py:145
  88.5 17.0 %all-to-all-start.3 = ((f32[64,2,128]{2,1,0:T(2,128)}), f32[64,2,128]{2,1,0:T(2,128)S(1)}, u32[]{:S(2)}, u32[]{:S(2)}) async-start(f32[64,2,128]{2,1,0:T(2,128)} %broadcast_in_dim.9), calls=%async_computation.3 | async-start | bytes 131072 | tf_op jit(solution)/shard_map/all_to_all | solution.py:123
  111.9 1.0 copy-start.2
  111.9 9.8 %collective-permute-start.2 = (f32[1024,128]{0,1:T(8,128)S(1)}, f32[1024,128]{0,1:T(8,128)S(1)}, u32[]{:S(2)}, u32[]{:S(2)}) collective-permute-start(f32[1024,128]{0,1:T(8,128)S(1)} %fusion.4), channel_id=1, source_target_pairs={{7,0},{0,1},{1,2},{2,3},{3,4},{4,5},{5,6},{6,7},{15,8},{8,9},{9,10... | collective-permute-start | bytes 1572872 | tf_op jit(solution)/shard_map/ppermute | solution.py:140
  122.9 16.8 %all-to-all-start.4 = ((f32[64,2,128]{2,1,0:T(2,128)}), f32[64,2,128]{2,1,0:T(2,128)S(1)}, u32[]{:S(2)}, u32[]{:S(2)}) async-start(f32[64,2,128]{2,1,0:T(2,128)} %bitcast.13), calls=%async_computation.4 | async-start | bytes 131072 | tf_op jit(solution)/shard_map/all_to_all | solution.py:121
  128.3 29.2 %collective-permute-start.3 = (f32[128,128]{1,0:T(8,128)S(1)}, f32[128,128]{1,0:T(8,128)S(1)}, u32[]{:S(2)}, u32[]{:S(2)}) collective-permute-start(f32[128,128]{1,0:T(8,128)S(1)} %slice_select_fusion.2), channel_id=1, source_target_pairs={{7,0},{0,1},{1,2},{2,3},{3,4},{4,5},{5,6},{6,7},{15,8},{8,9},{9,10... | collective-permute-start | bytes 196616 | tf_op jit(solution)/shard_map/ppermute | solution.py:145
  140.5 16.8 %all-to-all-start.5 = ((f32[64,2,128]{2,1,0:T(2,128)}), f32[64,2,128]{2,1,0:T(2,128)S(1)}, u32[]{:S(2)}, u32[]{:S(2)}) async-start(f32[64,2,128]{2,1,0:T(2,128)} %broadcast_in_dim.10), calls=%async_computation.5 | async-start | bytes 131072 | tf_op jit(solution)/shard_map/all_to_all | solution.py:123
  163.7 9.8 %collective-permute-start.4 = (f32[1024,128]{0,1:T(8,128)S(1)}, f32[1024,128]{0,1:T(8,128)S(1)}, u32[]{:S(2)}, u32[]{:S(2)}) collective-permute-start(f32[1024,128]{0,1:T(8,128)S(1)} %fusion.2), channel_id=1, source_target_pairs={{7,0},{0,1},{1,2},{2,3},{3,4},{4,5},{5,6},{6,7},{15,8},{8,9},{9,10... | collective-permute-start | bytes 1572872 | tf_op jit(solution)/shard_map/ppermute | solution.py:140
  174.8 5.4 %copy-start.3 = (f32[128,256]{1,0:T(8,128)S(1)}, f32[128,256]{1,0:T(8,128)}, u32[]{:S(2)}) copy-start(f32[128,256]{1,0:T(8,128)} %get-tuple-element.20) | copy-start | bytes 393220
  174.8 16.9 %all-to-all-start.6 = ((f32[64,2,128]{2,1,0:T(2,128)}), f32[64,2,128]{2,1,0:T(2,128)S(1)}, u32[]{:S(2)}, u32[]{:S(2)}) async-start(f32[64,2,128]{2,1,0:T(2,128)} %bitcast.20), calls=%async_computation.6 | async-start | bytes 131072 | tf_op jit(solution)/shard_map/all_to_all | solution.py:121
  180.2 29.1 %collective-permute-start.5 = (f32[128,128]{1,0:T(8,128)S(1)}, f32[128,128]{1,0:T(8,128)S(1)}, u32[]{:S(2)}, u32[]{:S(2)}) collective-permute-start(f32[128,128]{1,0:T(8,128)S(1)} %slice_select_fusion), channel_id=1, source_target_pairs={{7,0},{0,1},{1,2},{2,3},{3,4},{4,5},{5,6},{6,7},{15,8},{8,9},{9,10... | collective-permute-start | bytes 196616 | tf_op jit(solution)/shard_map/ppermute | solution.py:145
  192.4 16.8 %all-to-all-start.7 = ((f32[64,2,128]{2,1,0:T(2,128)}), f32[64,2,128]{2,1,0:T(2,128)S(1)}, u32[]{:S(2)}, u32[]{:S(2)}) async-start(f32[64,2,128]{2,1,0:T(2,128)} %broadcast_in_dim.11), calls=%async_computation.7 | async-start | bytes 131072 | tf_op jit(solution)/shard_map/all_to_all | solution.py:123
  216.2 9.8 %collective-permute-start.6 = (f32[1024,128]{0,1:T(8,128)S(1)}, f32[1024,128]{0,1:T(8,128)S(1)}, u32[]{:S(2)}, u32[]{:S(2)}) collective-permute-start(f32[1024,128]{0,1:T(8,128)S(1)} %fusion), channel_id=1, source_target_pairs={{7,0},{0,1},{1,2},{2,3},{3,4},{4,5},{5,6},{6,7},{15,8},{8,9},{9,10... | collective-permute-start | bytes 1572872 | tf_op jit(solution)/shard_map/ppermute | solution.py:140
